TPU v7x, 512 devices: a whole 4x4x16 slice. The times are simulated.
512 devices in a mesh: row: 32 (over x, z_lo, core), col: 16 (over y, z_hi).
Axes of the slice: x: 4, y: 4, z: 16 (z_hi: 4, z_lo: 4; z = z_hi * 4 + z_lo), core: 2. Of those that a mesh axis runs over, the one named last changes fastest.
Arguments:
- features: bfloat16 [65536, 256], P(('col', 'row')), may hold values from -6 to 6
- adjacency: bfloat16 [32, 16, 32, 128, 128], P('row', 'col'), may hold values from 0 to 0.109375, as said below
- block_rows: int32 [32, 16, 32], P('row', 'col'), may hold values from 0 to 15, as said below
- block_cols: int32 [32, 16, 32], P('row', 'col'), may hold values from 0 to 31
- block_count: int32 [32, 16], P('row', 'col'), may hold values from 1 to 32, as said below
- weight: bfloat16 [256, 256], replicated, may hold values from -3 to 3
- bias_term: float32 [256], replicated, may hold values from -3 to 3
- cotangent: bfloat16 [65536, 256], P(('row', 'col')), may hold values from -6 to 6
Outputs:
- hidden_out: bfloat16 [65536, 256], P(('row', 'col'))
- grad_weight: float32 [256, 256], replicated
- grad_bias: float32 [256], replicated
- grad_features: bfloat16 [65536, 256], P(('col', 'row'))
Inputs may be any that keep to these rules, and one draw needn't show every extreme that they name: `adjacency`: tiles are sparse with nonnegative entries. Within one grid cell the 32 slots name distinct pairs (block_rows, block_cols). The live slots of a cell are its first block_count slots; some cell is full.
All inputs are finite; a program needn't handle non-finite values.
Results may differ from a plain program's by a relative error of at most 0.02.
Values may be sent and summed in bfloat16 or wider, within the bound.
A program may use at most 64 MiB of HBM per device.

v0:
```python
import math

import jax
import jax.numpy as jnp
from jax import lax
from jax.sharding import PartitionSpec as P

H = 256
BS = 128


def gelu_exact(values):
    return jax.nn.gelu(values, approximate=False)


def accumulate(tile_set, source, source_ids, target_ids, live_count, target_count, transposed):
    slot_count = tile_set.shape[0]
    per_step = math.gcd(slot_count, 16)
    source_blocks = source.reshape(-1, BS, H)

    def advance(position, running):
        first_slot = position * per_step
        tile_group = lax.dynamic_slice_in_dim(tile_set, first_slot, per_step, 0)
        source_group = lax.dynamic_slice_in_dim(source_ids, first_slot, per_step, 0)
        target_group = lax.dynamic_slice_in_dim(target_ids, first_slot, per_step, 0)
        chosen = jnp.take(source_blocks, source_group, axis=0)
        if transposed:
            products = jnp.einsum(
                "gji,gjh->gih", tile_group, chosen, preferred_element_type=jnp.float32
            )
        else:
            products = jnp.einsum(
                "gij,gjh->gih", tile_group, chosen, preferred_element_type=jnp.float32
            )
        is_live = first_slot + jnp.arange(per_step, dtype=jnp.int32) < live_count
        products = jnp.where(is_live[:, None, None], products, 0.0)
        for slot in range(per_step):
            target = target_group[slot]
            current = lax.dynamic_slice_in_dim(running, target, 1, 0)
            running = lax.dynamic_update_slice_in_dim(
                running, current + products[slot][None], target, 0
            )
        return running

    last_step = slot_count // per_step
    empty = jnp.zeros((target_count, BS, H), jnp.float32)
    return lax.fori_loop(0, last_step, advance, empty).reshape(-1, H).astype(jnp.bfloat16)


def activate(aggregate, weight, bias_term, upstream):
    pre_act = jnp.dot(aggregate, weight, preferred_element_type=jnp.float32) + bias_term
    activated, pullback = jax.vjp(gelu_exact, pre_act)
    grad_pre = pullback(upstream.astype(jnp.float32))[0].astype(jnp.bfloat16)
    return (activated.astype(jnp.bfloat16), grad_pre)


def shards(features, adjacency, block_rows, block_cols, block_count, weight, bias_term, cotangent):
    tile_set = adjacency.reshape(adjacency.shape[2:])
    row_ids = block_rows.reshape(-1)
    col_ids = block_cols.reshape(-1)
    live_count = block_count.reshape(())
    rows_here = features.shape[0]
    n_row = lax.axis_size("row")
    n_col = lax.axis_size("col")
    feature_slab = lax.all_gather(features, "row", axis=0, tiled=True)
    partial_value = accumulate(
        tile_set, feature_slab, col_ids, row_ids, live_count, rows_here * n_col // BS, False
    )
    own_agg = (
        lax.psum_scatter(partial_value, "col", scatter_dimension=0, tiled=True)
        .astype(jnp.float32)
        .astype(jnp.bfloat16)
    )
    hidden_out, own_grad = activate(own_agg, weight, bias_term, cotangent)
    grad_agg = jnp.dot(own_grad, weight.T, preferred_element_type=jnp.float32).astype(jnp.bfloat16)
    grad_slab = lax.all_gather(grad_agg, "col", axis=0, tiled=True)
    local_weight = lax.dot_general(
        own_agg, own_grad, (((0,), (0,)), ((), ())), preferred_element_type=jnp.float32
    )
    local_bias = jnp.sum(own_grad.astype(jnp.float32), axis=0)
    total_weight, total_bias = lax.psum((local_weight, local_bias), ("row", "col"))
    factor = 1.0 / math.sqrt(rows_here * n_row * n_col)
    back = accumulate(
        tile_set, grad_slab, row_ids, col_ids, live_count, rows_here * n_row // BS, True
    )
    grad_features = (
        lax.psum_scatter(back, "row", scatter_dimension=0, tiled=True)
        .astype(jnp.float32)
        .astype(jnp.bfloat16)
    )
    return (hidden_out, total_weight * factor, total_bias * factor, grad_features)


def solution(mesh):
    return jax.shard_map(
        shards,
        mesh=mesh,
        in_specs=(
            P(("col", "row"), None),
            P("row", "col", None, None, None),
            P("row", "col", None),
            P("row", "col", None),
            P("row", "col"),
            P(),
            P(),
            P(("row", "col"), None),
        ),
        out_specs=(P(("row", "col"), None), P(), P(), P(("col", "row"), None)),
        check_vma=False,
    )
```

profile of v0, /device:TPU:1, one launch (start us, length us, event | category | flops | bytes accessed | tf_op | source)
XLA Modules:
  0.0 955.2 jit_solution(9541213911211515085)
XLA Ops:
  8.0 73.2 %all-gather.3.cloned.1.call-done = bf16[4096,256]{1,0:T(8,128)(2,1)} async-done(((bf16[128,256]{1,0:T(8,128)(2,1)}), bf16[4096,256]{1,0:T(8,128)(2,1)}) %all-gather.3.cloned.1.call-update) | async-done | bytes 2097168 | tf_op jit(solution)/shard_map/all_gather | solution.py:65
  81.4 72.0 %while.26 = (s32[]{:T(128)}, f32[16,128,256]{2,1,0:T(8,128)S(1)}, s32[32]{0:T(128)S(1)}, s32[]{:T(128)}, bf16[32,128,128]{2,1,0:T(8,128)(2,1)}, /*index=5*/s32[3...) while((s32[]{:T(128)}, f32[16,128,256]{2,1,0:T(8,128)S(1)}, ...), condition=%wide.region_1.0_spmd, body=%wide.region_0.1_spmd.sunk | while | flops 135791744 | bytes 12064079 | solution.py:47
  113.1 2.2 gather_fusion
  149.1 2.2 gather_fusion
  154.7 111.7 %reduce-scatter.3.cloned.1.call-done = bf16[128,256]{1,0:T(8,128)(2,1)} async-done(((bf16[2048,256]{1,0:T(8,128)(2,1)}), bf16[128,256]{1,0:T(8,128)(2,1)}) %reduce-scatter.3.cloned.1.call-update) | async-done | bytes 65552 | tf_op jit(solution)/shard_map/reduce_scatter | solution.py:70
  266.4 2.0 convert_reduce_fusion
  271.0 72.2 %all-gather.5.cloned.1.call-done = bf16[2048,256]{1,0:T(8,128)(2,1)} async-done(((bf16[128,256]{1,0:T(8,128)(2,1)}), bf16[2048,256]{1,0:T(8,128)(2,1)}) %all-gather.5.cloned.1.call-update) | async-done | bytes 1048592 | tf_op jit(solution)/shard_map/all_gather | solution.py:76
  343.2 2.4 broadcast_in_dim.110
  345.7 116.5 %while.27 = (s32[]{:T(128)}, f32[32,128,256]{2,1,0:T(8,128)}, s32[32]{0:T(128)S(1)}, s32[]{:T(128)}, bf16[32,128,128]{1,2,0:T(8,128)(2,1)S(1)}, /*index=5*/s32[3...) while((s32[]{:T(128)}, f32[32,128,256]{2,1,0:T(8,128)}, ...), condition=%wide.region_7.8_spmd, body=%wide.region_6.7_spmd.sunk | while | flops 135791744 | bytes 12066151 | solution.py:47
  378.7 1.6 fusion.128
  385.0 1.6 fusion.132
  386.6 1.6 fusion.133
  388.2 1.6 fusion.134
  389.7 1.6 fusion.135
  392.9 1.6 fusion.137
  396.0 1.6 fusion.139
  397.6 1.6 fusion.140
  400.8 1.6 fusion.142
  402.4 1.6 fusion.143
  441.7 1.6 fusion.131
  446.4 1.6 fusion.134
  448.0 1.6 fusion.135
  449.6 1.6 fusion.136
  451.1 1.6 fusion.137
  455.8 1.6 fusion.140
  457.4 1.6 fusion.141
  460.6 1.6 fusion.143
  462.2 3.8 convert_element_type.38
  466.7 102.2 %psum.15 = f32[256]{0:T(256)S(1)} all-reduce(f32[256]{0:T(256)S(1)} %copy-done.8), channel_id=1, replica_groups=mesh['row'=32,'col'=16] {'row','col'}, use_global_device_ids=true, to_apply=%region_5.6 | all-reduce | flops 256 | bytes 2048 | tf_op jit(solution)/shard_map/psum | solution.py:81
  570.1 230.4 %all-reduce.2.cloned.1.call-done = f32[256,256]{1,0:T(8,128)} async-done(((f32[256,256]{1,0:T(8,128)}), f32[256,256]{1,0:T(8,128)}) %all-reduce.2.cloned.1.call-update) | async-done | bytes 262160 | tf_op jit(solution)/shard_map/psum | solution.py:81
  800.5 1.7 broadcast_multiply_fusion
  802.2 146.5 %reduce-scatter.5.cloned.1.call-done = bf16[128,256]{1,0:T(8,128)(2,1)} async-done(((bf16[4096,256]{1,0:T(8,128)(2,1)}), bf16[128,256]{1,0:T(8,128)(2,1)}) %reduce-scatter.5.cloned.1.call-update) | async-done | bytes 65552 | tf_op jit(solution)/shard_map/reduce_scatter | solution.py:87
  (111 shorter events, 40.8 us)
Async XLA Ops:
  7.2 259.3 %copy-start = (bf16[256,256]{1,0:T(8,128)(2,1)S(1)}, bf16[256,256]{1,0:T(8,128)(2,1)}, u32[]{:S(2)}) copy-start(bf16[256,256]{1,0:T(8,128)(2,1)} %param.17) | copy-start | bytes 393220
  7.2 74.2 %copy-start.5 = (s32[1,1,32]{2,1,0:T(1,128)S(1)}, s32[1,1,32]{2,1,0:T(1,128)}, u32[]{:S(2)}) copy-start(s32[1,1,32]{2,1,0:T(1,128)} %param.15) | copy-start | bytes 388
  7.2 74.2 %copy-start.4 = (s32[1,1,32]{2,1,0:T(1,128)S(1)}, s32[1,1,32]{2,1,0:T(1,128)}, u32[]{:S(2)}) copy-start(s32[1,1,32]{2,1,0:T(1,128)} %param.14) | copy-start | bytes 388
  7.2 74.0 %all-gather.3.cloned.1.call-start = ((), (), s32[]{:S(2)}) async-start(), calls=%async_computation.2 | async-start | bytes 2162688 | tf_op jit(solution)/shard_map/all_gather | solution.py:65
  7.9 258.5 %reduce-scatter.3.cloned.1.call-start = ((), (), s32[]{:S(2)}) async-start(), calls=%async_computation.3 | async-start | bytes 1114112 | tf_op jit(solution)/shard_map/reduce_scatter | solution.py:70
  153.5 113.0 %copy-start.9 = (bf16[128,256]{1,0:T(8,128)(2,1)S(1)}, bf16[128,256]{1,0:T(8,128)(2,1)}, u32[]{:S(2)}) copy-start(bf16[128,256]{1,0:T(8,128)(2,1)} %param.19) | copy-start | bytes 196612
  153.5 113.0 %copy-start.10 = (f32[256]{0:T(256)S(1)}, f32[256]{0:T(256)}, u32[]{:S(2)}) copy-start(f32[256]{0:T(256)} %param.18) | copy-start | bytes 3076
  154.6 114.7 %copy-start.2 = (bf16[32,128,128]{2,1,0:T(8,128)(2,1)S(1)}, bf16[32,128,128]{2,1,0:T(8,128)(2,1)}, u32[]{:S(2)}) copy-start(bf16[32,128,128]{2,1,0:T(8,128)(2,1)} %get-tuple-element.566) | copy-start | bytes 3145732
  154.6 188.6 %all-gather.5.cloned.1.call-start = ((), (), s32[]{:S(2)}) async-start(), calls=%async_computation.5 | async-start | bytes 1114112 | tf_op jit(solution)/shard_map/all_gather | solution.py:76
  266.4 3.6 copy-start.3
  269.3 531.2 %all-reduce.2.cloned.1.call-start = ((), (), s32[]{:S(2)}) async-start(), calls=%async_computation.4 | async-start | bytes 524288 | tf_op jit(solution)/shard_map/psum | solution.py:81
  270.9 677.8 %reduce-scatter.5.cloned.1.call-start = ((), (), s32[]{:S(2)}) async-start(), calls=%async_computation.6 | async-start | bytes 2162688 | tf_op jit(solution)/shard_map/reduce_scatter | solution.py:87
  343.2 2.5 copy-start.1
  345.7 0.8 copy-start.6
  386.6 17.4 %copy-start.7 = (s32[32]{0:T(128)S(1)}, s32[32]{0:T(128)}, u32[]{:S(2)}) copy-start(s32[32]{0:T(128)} %copy-done.6) | copy-start | bytes 388 | tf_op jit(solution)/shard_map/while
  403.9 0.8 copy-start.6
  444.8 17.4 %copy-start.7 = (s32[32]{0:T(128)S(1)}, s32[32]{0:T(128)}, u32[]{:S(2)}) copy-start(s32[32]{0:T(128)} %copy-done.6) | copy-start | bytes 388 | tf_op jit(solution)/shard_map/while
  466.0 0.7 copy-start.8
Sparse Core Ops, SparseCore 0:
  10.2 70.9 all-gather.2
  154.8 111.6 reduce-scatter.2
  270.5 72.7 all-gather.4
  350.0 450.4 all-reduce.1
  803.7 144.9 reduce-scatter.4
where the time goes:
time: 962 us; the launch traced here: 955 us
  waiting for transfers between devices  635 us (66%)
  loops' own time  121 us (13%)
  blocking collectives  102 us (11%)
  other arithmetic  62 us (6%)
  between operations  13.9 us (1%)
  local copies, waits for them, and re-layouts  12.8 us (1%)
    psum x1, waiting for transfers between devices, shards(): lax.psum((local_weight, local_bias), ('row', 'col'))  230 us
    reduce_scatter x1, waiting for transfers between devices, shards(): lax.psum_scatter(back, 'row', scatter_dimension=0, tiled=True)  147 us
    another operation x2, loops' own time, accumulate(): lax.fori_loop(0, last_step, advance, empty).reshape(-1, H)  121 us
    reduce_scatter x1, waiting for transfers between devices, shards(): lax.psum_scatter(partial_value, 'col', scatter_dimension=0, tiled=True)  112 us
    psum x1, blocking collectives, shards(): lax.psum((local_weight, local_bias), ('row', 'col'))  102 us
    all_gather x1, waiting for transfers between devices, shards(): feature_slab = lax.all_gather(features, 'row', axis=0, tiled=True)  73.2 us
    all_gather x1, waiting for transfers between devices, shards(): grad_slab = lax.all_gather(grad_agg, 'col', axis=0, tiled=True)  72.2 us
    dynamic_update_slice x64, other arithmetic, advance(): lax.dynamic_update_slice_in_dim(running, current + products[slot][None],...  51.3 us
  transfers between devices with their start and end apart: 5, of which 5 were waited for; matrix products, arithmetic and copies ran while one was open for 7% of the time, Pallas kernels for 0%

commit v1 on v0

v1 whole, which is shorter than its diff:
```python
import math

import jax
import jax.numpy as jnp
from jax import lax
from jax.experimental import pallas as pl
from jax.experimental.pallas import tpu as pltpu
from jax.sharding import PartitionSpec as P

H = 256
BS = 128
HALF = BS // 2
SLOTS = 32
TILE_ROWS = 16
TILE_COLS = 32
NODES = 65536
COPIES = 192
INV_SQRT2 = math.sqrt(0.5)
INV_SQRT_2PI = 1.0 / math.sqrt(2.0 * math.pi)


def f32(value):
    return value.astype(jnp.float32)


def chain_tables(keys, live, prev, last, targets):
    def prev_of(k, carry):
        key = keys[k]
        found = jnp.int32(0)
        for j in range(SLOTS - 1):
            hit = (keys[j] == key) & (j < k) & (j < live)
            found = jnp.where(hit, j + 1, found)
        prev[k] = found
        return carry

    lax.fori_loop(0, SLOTS, prev_of, 0)

    def last_of(t, carry):
        found = jnp.int32(0)
        for j in range(SLOTS):
            found = jnp.where((keys[j] == t) & (j < live), j + 1, found)
        last[t] = found
        return carry

    lax.fori_loop(0, targets, last_of, 0)


def kernel(
    features, adjacency, block_rows, block_cols, block_count, weight, bias_term, cotangent,
    hidden_out, weight_out, bias_out, features_out,
    tiles, slab, wgt, bias, cot, chain, part, gslab, back,
    prev_f, last_f, prev_b, last_b,
    y2p, y2m, ysp, ysm, yp_in, ym_in, mid,
    z2p, z2m, zsp, zsm, zp_in, zm_in,
    core_in, xsum, x2p, x2m, xsp, xsm, xp_in, xm_in, zout, zin,
    hid, fin, w0, w0_in, w1, w1_in, w2, w2_in, w3_in, w4_in, wfin, bfin,
    local_sem, send_sem, recv_sem,
):
    row = lax.axis_index("row")
    col = lax.axis_index("col")
    x, zl, core = row // 8, (row // 2) % 4, row % 2
    y, zh = col // 4, col % 4
    other = 1 - core
    xp, xm, x2 = (x + 1) % 4, (x + 3) % 4, (x + 2) % 4
    yp, ym, y2 = (y + 1) % 4, (y + 3) % 4, (y + 2) % 4
    zhp, zhm, zh2 = (zh + 1) % 4, (zh + 3) % 4, (zh + 2) % 4
    zl1, zl2, zl3 = zl + 1 - 2 * (zl % 2), (zl + 2) % 4, 3 - zl

    def at_row(x_=None, zl_=None, core_=None):
        x_ = x if x_ is None else x_
        zl_ = zl if zl_ is None else zl_
        core_ = core if core_ is None else core_
        return (x_ * 8 + zl_ * 2 + core_, col)

    def at_col(y_=None, zh_=None):
        y_ = y if y_ is None else y_
        zh_ = zh if zh_ is None else zh_
        return (row, y_ * 4 + zh_)

    def block_of(x_, zl_, core_):
        return x_ * 8 + zl_ * 2 + core_

    started = []

    def send(src, dst, to):
        i = len(started)
        copy = pltpu.make_async_remote_copy(
            src_ref=src, dst_ref=dst, send_sem=send_sem.at[i], recv_sem=recv_sem.at[i],
            device_id=to, device_id_type=pl.DeviceIdType.MESH,
        )
        copy.start()
        started.append(copy)
        return copy

    locals_started = []

    def local(src, dst):
        copy = pltpu.make_async_copy(src, dst, local_sem.at[len(locals_started)])
        copy.start()
        locals_started.append(copy)
        return copy

    own = block_of(x, zl, core)
    own_in = local(features, slab.at[own])
    tiles_in = local(adjacency, tiles)
    wgt_in = local(weight, wgt)
    bias_in = local(bias_term, bias)
    cot_in = local(cotangent, cot)

    peers = (
        [at_row(zl_=z) for z in (zl1, zl2, zl3)]
        + [at_row(x_=v) for v in (xp, xm, x2)]
        + [at_row(core_=other)]
        + [at_col(y_=v) for v in (yp, ym, y2)]
        + [at_col(zh_=v) for v in (zhp, zhm, zh2)]
    )
    barrier = pltpu.get_barrier_semaphore()
    for peer in peers:
        pl.semaphore_signal(barrier, inc=1, device_id=peer, device_id_type=pl.DeviceIdType.MESH)
    pl.semaphore_wait(barrier, len(peers))

    own_in.wait()
    z_in = [send(slab.at[own], slab.at[own], at_row(zl_=z)) for z in (zl1, zl2, zl3)]
    from_m, from_p, sib = [], [], []
    chunks = (zl, zl1, zl2, zl3)

    def relay(b):
        from_m.append(send(slab.at[b], slab.at[b], at_row(x_=xp)))
        from_p.append(send(slab.at[b], slab.at[b], at_row(x_=xm)))
        sib.append(send(slab.at[b], slab.at[b], at_row(core_=other)))

    relay(own)
    live = block_count[0]
    chain[0] = jnp.zeros((BS, H), jnp.float32)
    chain_tables(block_rows, live, prev_f, last_f, TILE_ROWS)
    for c in range(1, 4):
        z_in[c - 1].wait_recv()
        relay(block_of(x, chunks[c], core))
    lower, upper = pl.ds(0, HALF), pl.ds(HALF, HALF)
    far = []
    for c in range(4):
        from_m[c].wait_recv()
        b = block_of(xm, chunks[c], core)
        lo = send(slab.at[b, lower], slab.at[b, lower], at_row(x_=xp))
        sib.append(send(slab.at[b], slab.at[b], at_row(core_=other)))
        from_p[c].wait_recv()
        b = block_of(xp, chunks[c], core)
        hi = send(slab.at[b, upper], slab.at[b, upper], at_row(x_=xm))
        sib.append(send(slab.at[b], slab.at[b], at_row(core_=other)))
        far.append((lo, hi))
    for c in range(4):
        far[c][0].wait_recv()
        far[c][1].wait_recv()
        b = block_of(x2, chunks[c], core)
        sib.append(send(slab.at[b], slab.at[b], at_row(core_=other)))
    tiles_in.wait()
    for copy in sib:
        copy.wait_recv()

    def forward_slot(k, carry):
        product = jnp.dot(tiles[k], slab[block_cols[k]], preferred_element_type=jnp.float32)
        chain[k + 1] = product + chain[prev_f[k]]
        return carry

    lax.fori_loop(0, SLOTS, forward_slot, 0, unroll=4)

    def place(t):
        part[t] = chain[last_f[t]].astype(jnp.bfloat16)

    order = (zh2, zhp, zhm, zh)
    m2p, m2m, d1p, d1m, s1p, s1m = [], [], [], [], [], []
    for b in order:
        t = y2 * 4 + b
        place(t)
        m2p.append(send(part.at[t, lower], y2p.at[b], at_col(y_=yp)))
        m2m.append(send(part.at[t, upper], y2m.at[b], at_col(y_=ym)))
    for b in order:
        t = yp * 4 + b
        place(t)
        d1p.append(send(part.at[t, upper], yp_in.at[b, upper], at_col(y_=yp)))
        t = ym * 4 + b
        place(t)
        d1m.append(send(part.at[t, lower], ym_in.at[b, lower], at_col(y_=ym)))
    for b in order:
        place(y * 4 + b)
    for i, b in enumerate(order):
        m2p[i].wait_recv()
        ysp[b] = (f32(part[yp * 4 + b, lower]) + f32(y2p[b])).astype(jnp.bfloat16)
        s1p.append(send(ysp.at[b], yp_in.at[b, lower], at_col(y_=yp)))
        m2m[i].wait_recv()
        ysm[b] = (f32(part[ym * 4 + b, upper]) + f32(y2m[b])).astype(jnp.bfloat16)
        s1m.append(send(ysm.at[b], ym_in.at[b, upper], at_col(y_=ym)))

    def y_total(i):
        b = order[i]
        for copies in (d1p, d1m, s1p, s1m):
            copies[i].wait_recv()
        mid[b] = (f32(part[y * 4 + b]) + f32(yp_in[b]) + f32(ym_in[b])).astype(jnp.bfloat16)

    y_total(0)
    zm2p = send(mid.at[zh2, lower], z2p, at_col(zh_=zhp))
    zm2m = send(mid.at[zh2, upper], z2m, at_col(zh_=zhm))
    y_total(1)
    zd1p = send(mid.at[zhp, upper], zp_in.at[upper], at_col(zh_=zhp))
    y_total(2)
    zd1m = send(mid.at[zhm, lower], zm_in.at[lower], at_col(zh_=zhm))
    y_total(3)
    zm2p.wait_recv()
    zsp[...] = (f32(mid[zhp, lower]) + f32(z2p[...])).astype(jnp.bfloat16)
    zs1p = send(zsp, zp_in.at[lower], at_col(zh_=zhp))
    zm2m.wait_recv()
    zsm[...] = (f32(mid[zhm, upper]) + f32(z2m[...])).astype(jnp.bfloat16)
    zs1m = send(zsm, zm_in.at[upper], at_col(zh_=zhm))
    chain_tables(block_cols, live, prev_b, last_b, TILE_COLS)
    for copy in (wgt_in, bias_in, cot_in):
        copy.wait()
    for copy in (zd1p, zd1m, zs1p, zs1m):
        copy.wait_recv()
    agg = (f32(mid[zh]) + f32(zp_in[...]) + f32(zm_in[...])).astype(jnp.bfloat16)

    pre = jnp.dot(agg, wgt[...], preferred_element_type=jnp.float32) + bias[...]
    cdf = 0.5 * (1.0 + lax.erf(pre * INV_SQRT2))
    slope = cdf + pre * (jnp.exp(-0.5 * pre * pre) * INV_SQRT_2PI)
    grad_pre = (f32(cot[...]) * slope).astype(jnp.bfloat16)
    gslab[col] = lax.dot_general(
        grad_pre, wgt[...], (((1,), (1,)), ((), ())), preferred_element_type=jnp.float32
    ).astype(jnp.bfloat16)

    gz_m = send(gslab.at[col], gslab.at[col], at_col(zh_=zhp))
    gz_p = send(gslab.at[col], gslab.at[col], at_col(zh_=zhm))
    gy_m, gy_p = [], []

    def spread(b):
        gy_m.append(send(gslab.at[b], gslab.at[b], at_col(y_=yp)))
        gy_p.append(send(gslab.at[b], gslab.at[b], at_col(y_=ym)))

    spread(col)
    hid[...] = (pre * cdf).astype(jnp.bfloat16)
    hid_out = local(hid, hidden_out)
    grad_w = lax.dot_general(agg, grad_pre, (((0,), (0,)), ((), ())), preferred_element_type=jnp.float32)
    w0[0, 0:128] = grad_w[0:128]
    w0[1, 0:128] = grad_w[128:256]
    grad_b = jnp.broadcast_to(jnp.sum(f32(grad_pre), axis=0, keepdims=True), (8, H))
    w0[0, 128:136] = grad_b
    w0[1, 128:136] = grad_b
    wc = send(w0.at[other], w0_in, at_row(core_=other))

    gz_m.wait_recv()
    b = y * 4 + zhm
    gz2_lo = send(gslab.at[b, lower], gslab.at[b, lower], at_col(zh_=zhp))
    spread(b)
    gz_p.wait_recv()
    b = y * 4 + zhp
    gz2_hi = send(gslab.at[b, upper], gslab.at[b, upper], at_col(zh_=zhm))
    spread(b)

    wc.wait_recv()
    w_core = w0[core] + w0_in[...]
    for v in range(4):
        w1[v, 0:32] = w_core[32 * v : 32 * v + 32]
        w1[v, 32:40] = w_core[128:136]
    w1_in[x] = w1[x]
    wx = [send(w1.at[v], w1_in.at[x], at_row(x_=v)) for v in (xp, xm, x2)]

    g_far = []

    def spread_far(i):
        gy_m[i].wait_recv()
        b = ym * 4 + g_order[i]
        lo = send(gslab.at[b, lower], gslab.at[b, lower], at_col(y_=yp))
        gy_p[i].wait_recv()
        b = yp * 4 + g_order[i]
        hi = send(gslab.at[b, upper], gslab.at[b, upper], at_col(y_=ym))
        g_far.append((lo, hi))

    g_order = (zh, zhm, zhp, zh2)
    spread_far(0)
    gz2_lo.wait_recv()
    gz2_hi.wait_recv()
    spread(y * 4 + zh2)
    for i in range(1, 3):
        spread_far(i)
    for copy in wx:
        copy.wait_recv()
    w_x = w1_in[0] + w1_in[1] + w1_in[2] + w1_in[3]
    for v in range(4):
        w2[v, 0:8] = w_x[8 * v : 8 * v + 8]
        w2[v, 8:16] = w_x[32:40]
    w2_in[zl] = w2[zl]
    wz = [send(w2.at[v], w2_in.at[zl], at_row(zl_=v)) for v in (zl1, zl2, zl3)]
    spread_far(3)
    for pair in g_far:
        pair[0].wait_recv()
        pair[1].wait_recv()

    def backward_slot(k, carry):
        product = lax.dot_general(
            tiles[k], gslab[block_rows[k]], (((0,), (0,)), ((), ())), preferred_element_type=jnp.float32
        )
        chain[k + 1] = product + chain[prev_b[k]]
        return carry

    lax.fori_loop(0, SLOTS, backward_slot, 0, unroll=4)

    def place_back(t):
        back[t] = chain[last_b[t]].astype(jnp.bfloat16)

    zs = (zl, zl1, zl2, zl3)
    core_copies = {}
    for name, v in (("x2", x2), ("xp", xp), ("xm", xm), ("x", x)):
        for i, z in enumerate(zs):
            t = block_of(v, z, other)
            place_back(t)
            core_copies[name, i] = send(back.at[t], core_in.at[v * 4 + z], at_row(core_=other))
            place_back(block_of(v, z, core))

    for copy in wz:
        copy.wait_recv()
    w_z = w2_in[0] + w2_in[1] + w2_in[2] + w2_in[3]
    w3_in[y] = w_z
    wy = [send(w3_in.at[y], w3_in.at[y], at_col(y_=v)) for v in (yp, ym, y2)]

    def core_total(name, v, i):
        z = zs[i]
        core_copies[name, i].wait_recv()
        s = f32(back[block_of(v, z, core)]) + f32(core_in[v * 4 + z])
        xsum[v * 4 + z] = s.astype(jnp.bfloat16)

    m2p, m2m, d1p, d1m, s1p, s1m = [], [], [], [], [], []
    for i, z in enumerate(zs):
        core_total("x2", x2, i)
        m2p.append(send(xsum.at[x2 * 4 + z, lower], x2p.at[z], at_row(x_=xp)))
        m2m.append(send(xsum.at[x2 * 4 + z, upper], x2m.at[z], at_row(x_=xm)))
    for i, z in enumerate(zs):
        core_total("xp", xp, i)
        d1p.append(send(xsum.at[xp * 4 + z, upper], xp_in.at[z, upper], at_row(x_=xp)))
        core_total("xm", xm, i)
        d1m.append(send(xsum.at[xm * 4 + z, lower], xm_in.at[z, lower], at_row(x_=xm)))
    for i, z in enumerate(zs):
        core_total("x", x, i)

    for copy in wy:
        copy.wait_recv()
    w_y = w3_in[0] + w3_in[1] + w3_in[2] + w3_in[3]
    w4_in[zh] = w_y
    wh = [send(w4_in.at[zh], w4_in.at[zh], at_col(zh_=v)) for v in (zhp, zhm, zh2)]

    for i, z in enumerate(zs):
        m2p[i].wait_recv()
        xsp[z] = (f32(xsum[xp * 4 + z, lower]) + f32(x2p[z])).astype(jnp.bfloat16)
        s1p.append(send(xsp.at[z], xp_in.at[z, lower], at_row(x_=xp)))
        m2m[i].wait_recv()
        xsm[z] = (f32(xsum[xm * 4 + z, upper]) + f32(x2m[z])).astype(jnp.bfloat16)
        s1m.append(send(xsm.at[z], xm_in.at[z, upper], at_row(x_=xm)))

    for copy in wh:
        copy.wait_recv()
    factor = 1.0 / math.sqrt(NODES)
    w_all = (w4_in[0] + w4_in[1] + w4_in[2] + w4_in[3]) * factor
    bfin[...] = w_all[8:9]
    mine = core * 16 + x * 4 + zl
    wfin[mine] = w_all[0:8]
    b_out = local(bfin, bias_out)
    wgz = [send(wfin.at[mine], wfin.at[mine], at_row(zl_=v)) for v in (zl1, zl2, zl3)]

    z_final = []
    for i in (2, 3, 1, 0):
        z = zs[i]
        for copies in (d1p, d1m, s1p, s1m):
            copies[i].wait_recv()
        s = f32(xsum[x * 4 + z]) + f32(xp_in[z]) + f32(xm_in[z])
        zout[i] = s.astype(jnp.bfloat16)
        if i > 0:
            z_final.append(send(zout.at[i], zin.at[i], at_row(zl_=z)))

    for copy in wgz:
        copy.wait_recv()
    quarter = pl.ds(core * 16 + x * 4, 4)
    wgx = [send(wfin.at[quarter], wfin.at[quarter], at_row(x_=v)) for v in (xp, xm, x2)]
    for copy in z_final:
        copy.wait_recv()
    total = f32(zout[0]) + f32(zin[1]) + f32(zin[2]) + f32(zin[3])
    fin[...] = total.astype(jnp.bfloat16)
    fin_out = local(fin, features_out)
    for copy in wgx:
        copy.wait_recv()
    half = pl.ds(core * 16, 16)
    wgc = send(wfin.at[half], wfin.at[half], at_row(core_=other))
    wgc.wait_recv()
    w_out = local(wfin, weight_out)
    for copy in started:
        copy.wait_send()
    for copy in (hid_out, b_out, fin_out, w_out):
        copy.wait()


def shards(features, adjacency, block_rows, block_cols, block_count, weight, bias_term, cotangent):
    bf16, fp32 = jnp.bfloat16, jnp.float32
    vmem = pltpu.VMEM
    hbm = pl.BlockSpec(memory_space=pl.ANY)
    smem = pl.BlockSpec(memory_space=pltpu.SMEM)
    scratch = [
        vmem((SLOTS, BS, BS), bf16),
        vmem((TILE_COLS, BS, H), bf16),
        vmem((H, H), bf16),
        vmem((1, H), fp32),
        vmem((BS, H), bf16),
        vmem((SLOTS + 1, BS, H), fp32),
        vmem((TILE_ROWS, BS, H), bf16),
        vmem((TILE_ROWS, BS, H), bf16),
        vmem((TILE_COLS, BS, H), bf16),
        pltpu.SMEM((SLOTS,), jnp.int32),
        pltpu.SMEM((TILE_ROWS,), jnp.int32),
        pltpu.SMEM((SLOTS,), jnp.int32),
        pltpu.SMEM((TILE_COLS,), jnp.int32),
    ]
    scratch += [vmem((4, HALF, H), bf16)] * 4 + [vmem((4, BS, H), bf16)] * 3
    scratch += [vmem((HALF, H), bf16)] * 4 + [vmem((BS, H), bf16)] * 2
    scratch += [vmem((16, BS, H), bf16)] * 2
    scratch += [vmem((4, HALF, H), bf16)] * 4 + [vmem((4, BS, H), bf16)] * 4
    scratch += [vmem((BS, H), bf16)] * 2
    scratch += [
        vmem((2, 136, H), fp32),
        vmem((136, H), fp32),
        vmem((4, 40, H), fp32),
        vmem((4, 40, H), fp32),
        vmem((4, 16, H), fp32),
        vmem((4, 16, H), fp32),
        vmem((4, 16, H), fp32),
        vmem((4, 16, H), fp32),
        vmem((32, 8, H), fp32),
        vmem((1, H), fp32),
        pltpu.SemaphoreType.DMA((16,)),
        pltpu.SemaphoreType.DMA((COPIES,)),
        pltpu.SemaphoreType.DMA((COPIES,)),
    ]
    hidden, grad_weight, grad_bias, grad_features = pl.pallas_call(
        kernel,
        out_shape=(
            jax.ShapeDtypeStruct((BS, H), bf16),
            jax.ShapeDtypeStruct((32, 8, H), fp32),
            jax.ShapeDtypeStruct((1, H), fp32),
            jax.ShapeDtypeStruct((BS, H), bf16),
        ),
        in_specs=[hbm, hbm, smem, smem, smem, hbm, hbm, hbm],
        out_specs=(hbm, hbm, hbm, hbm),
        scratch_shapes=scratch,
        compiler_params=pltpu.CompilerParams(
            collective_id=0, has_side_effects=True, vmem_limit_bytes=48 * 1024 * 1024
        ),
        name="gcn_layer",
    )(
        features,
        adjacency.reshape(SLOTS, BS, BS),
        block_rows.reshape(SLOTS),
        block_cols.reshape(SLOTS),
        block_count.reshape(1),
        weight,
        bias_term.reshape(1, H),
        cotangent,
    )
    return hidden, grad_weight.reshape(H, H), grad_bias.reshape(H), grad_features


def solution(mesh):
    return jax.shard_map(
        shards,
        mesh=mesh,
        in_specs=(
            P(("col", "row"), None),
            P("row", "col", None, None, None),
            P("row", "col", None),
            P("row", "col", None),
            P("row", "col"),
            P(),
            P(),
            P(("row", "col"), None),
        ),
        out_specs=(P(("row", "col"), None), P(), P(), P(("col", "row"), None)),
        check_vma=False,
    )
```

time: 962 us -> 116 us (0.12)
  waiting for transfers between devices: 635 us -> 0 us
  loops' own time: 121 us -> 0 us
  Pallas kernels: 0 us -> 107 us
  blocking collectives: 102 us -> 0 us
  other arithmetic: 62 us -> 0 us
  between operations: 13.9 us -> 1.32 us
    reduce_scatter x2 -> x0, waiting for transfers between devices: 258 us -> none  [the longest x1 147 us: shards(): lax.psum_scatter(back, 'row', scatter_dimension=0, tiled=True)]
    psum x1 -> x0, waiting for transfers between devices: 230 us -> none  [shards(): lax.psum((local_weight, local_bias), ('row', 'col'))]
    all_gather x2 -> x0, waiting for transfers between devices: 145 us -> none  [the longest x1 73.2 us: shards(): feature_slab = lax.all_gather(features, 'row', axis=0, tiled=True)]
    another operation x2 -> x0, loops' own time: 121 us -> none  [accumulate(): lax.fori_loop(0, last_step, advance, empty).reshape(-1, H)]
    pallas_call x0 -> x1, Pallas kernels: none -> 107 us  [shards(): pl.pallas_call(kernel, out_shape=(jax.ShapeDtypeStruct((BS, H), bf16), ja...]
    psum x1 -> x0, blocking collectives: 102 us -> none  [shards(): lax.psum((local_weight, local_bias), ('row', 'col'))]
    dynamic_update_slice x64 -> x0, other arithmetic: 51.3 us -> none  [advance(): lax.dynamic_update_slice_in_dim(running, current + products[slot][None],...]
  transfers between devices with their start and end apart: 5 -> 0, of which waited for: 5 -> 0; matrix products, arithmetic and copies ran while one was open for 7% -> 0% of each run, Pallas kernels for 0% -> 0%
where the time goes in v1:
time: 116 us; the launch traced here: 115 us
  Pallas kernels  107 us (92%)
  local copies, waits for them, and re-layouts  7.01 us (6%)
  between operations  1.32 us (1%)
    pallas_call x1, Pallas kernels, shards(): pl.pallas_call(kernel, out_shape=(jax.ShapeDtypeStruct((BS, H), bf16), ja...  107 us
    unnamed x18, local copies, waits for them, and re-layouts  7.01 us

profile of v1, /device:TPU:1, one launch (start us, length us, event | category | flops | bytes accessed | tf_op | source)
XLA Modules:
  0.0 115.3 jit_solution(16716711711454769098)
XLA Ops:
  1.3 0.0 copy-start.6
  1.3 0.0 copy-start.4
  1.3 0.0 copy-start.5
  1.3 0.6 copy-done.6
  1.9 0.0 copy-done.4
  2.0 0.0 copy-done.5
  2.0 0.0 copy-start
  2.0 1.2 %copy-done = bf16[1,1,32,128,128]{4,3,2,1,0:T(8,128)(2,1)S(1)} copy-done((bf16[1,1,32,128,128]{4,3,2,1,0:T(8,128)(2,1)S(1)}, bf16[1,1,32,128,128]{4,3,2,1,0:T(8,128)(2,1)}, u32[]{:S(2)}) %copy-start) | copy-done | bytes 1048600
  3.2 0.0 copy-start.1
  3.2 0.9 copy-done.1
  4.1 0.0 copy-start.2
  4.1 0.8 copy-done.2
  4.9 0.0 copy-start.3
  5.0 0.8 copy-done.3
  5.8 106.9 %gcn_layer.1 = (bf16[128,256]{1,0:T(8,128)(2,1)S(1)}, f32[32,8,256]{2,1,0:T(8,128)S(1)}, f32[1,256]{1,0:T(1,128)S(1)}, bf16[128,256]{1,0:T(8,128)(2,1)S(1)}) custom-call(bf16[128,256]{1,0:T(8,128)(2,1)S(1)} %copy-done.2, bf16[32,128,128]{2,1,0:T(8,128)(2,1)S(1)} %bitcast.8, s32[32]{0:T(128)S(1)} %bitcast.12, s32[32]{0:T(128)S(1)} %bitcast.13, ...), custom_call_target="tpu_custom_call" | custom-call | tf_op jit(solution)/shard_map/gcn_layer/pallas_call | solution.py:437
  112.7 0.6 copy.17
  113.4 0.7 copy.18
  114.1 0.6 copy.19
  114.6 0.6 copy.20
Async XLA Ops:
  1.3 0.7 copy-start.6
  1.3 0.7 copy-start.4
  1.3 0.7 copy-start.5
  2.0 1.2 %copy-start = (bf16[1,1,32,128,128]{4,3,2,1,0:T(8,128)(2,1)S(1)}, bf16[1,1,32,128,128]{4,3,2,1,0:T(8,128)(2,1)}, u32[]{:S(2)}) copy-start(bf16[1,1,32,128,128]{4,3,2,1,0:T(8,128)(2,1)} %param.9) | copy-start | bytes 3145732
  3.2 0.9 copy-start.1
  4.1 0.8 copy-start.2
  4.9 0.8 copy-start.3

commit v2 on v0

v2 whole, which is shorter than its diff:
```python
import math

import jax
import jax.numpy as jnp
from jax import lax
from jax.experimental import pallas as pl
from jax.experimental.pallas import tpu as pltpu
from jax.sharding import PartitionSpec as P

H = 256
BS = 128
COLS = 128
SLOTS = 32
TILE_ROWS = 16
TILE_COLS = 32
NODES = 65536
GROUP = 4
LOCALS = 14
SENDS = 16
RECVS = 66
INV_SQRT2 = math.sqrt(0.5)
INV_SQRT_2PI = 1.0 / math.sqrt(2.0 * math.pi)


def f32(value):
    return value.astype(jnp.float32)


def bf16(value):
    return value.astype(jnp.bfloat16)


def chain_tables(keys, live, prev, last, targets):
    def prev_of(k, carry):
        key = keys[k]
        found = jnp.int32(0)
        for j in range(SLOTS - 1):
            hit = (keys[j] == key) & (j < k) & (j < live)
            found = jnp.where(hit, j + 1, found)
        prev[k] = found
        return carry

    lax.fori_loop(0, SLOTS, prev_of, 0)

    def last_of(t, carry):
        found = jnp.int32(0)
        for j in range(SLOTS):
            found = jnp.where((keys[j] == t) & (j < live), j + 1, found)
        last[t] = found
        return carry

    lax.fori_loop(0, targets, last_of, 0)


def layer_kernel(
    features, adjacency, block_rows, block_cols, block_count, weight, bias_term, cotangent,
    hidden_out, weight_out, bias_out, features_out,
    tiles, wgt, bias, cot, chain, slab_a, slab_b, part, y_in, mid, zh_in, gslab_a, gslab_b, back, core_in, xsum, x_in, zl_out, zl_in,
    hid, fin, w0, w0_in, w1, w1_in, w2, w2_in, w3_in, w4_in, wfin, bfin,
    rows_s, cols_s, count_s, prev_f, last_f, prev_b, last_b,
    local_sem, send_sem, recv_sem,
):
    slab, gslab = (slab_a, slab_b), (gslab_a, gslab_b)
    row = lax.axis_index("row")
    col = lax.axis_index("col")
    x, zl, core = row // 8, (row // 2) % 4, row % 2
    y, zh = col // 4, col % 4
    other = 1 - core
    xs = ((x + 2) % 4, (x + 1) % 4, (x + 3) % 4)
    ys = ((y + 2) % 4, (y + 1) % 4, (y + 3) % 4)
    zhs = ((zh + 2) % 4, (zh + 1) % 4, (zh + 3) % 4)
    zls = ((zl + 2) % 4, 3 - zl, zl + 1 - 2 * (zl % 2))

    def block_of(x_, zl_, core_):
        return x_ * 8 + zl_ * 2 + core_

    def at_x(x_):
        return (block_of(x_, zl, core), col)

    def at_zl(zl_):
        return (block_of(x, zl_, core), col)

    def at_y(y_):
        return (row, y_ * 4 + zh)

    def at_zh(zh_):
        return (row, y * 4 + zh_)

    sibling = (block_of(x, zl, other), col)
    counts = {"send": 0, "recv": 0, "local": 0}

    def new(kind):
        counts[kind] += 1
        return counts[kind] - 1

    def send(src, dst, to, s, r):
        pltpu.make_async_remote_copy(
            src_ref=src, dst_ref=dst, send_sem=send_sem.at[s], recv_sem=recv_sem.at[r],
            device_id=to, device_id_type=pl.DeviceIdType.MESH,
        ).start()

    def whole(ref, s, r):
        return pltpu.make_async_remote_copy(
            src_ref=ref, dst_ref=ref, send_sem=send_sem.at[s], recv_sem=recv_sem.at[r],
            device_id=sibling, device_id_type=pl.DeviceIdType.MESH,
        )

    def arrived(r, ref):
        whole(ref, 0, r).wait_recv()

    def left(s, ref):
        whole(ref, s, 0).wait_send()

    def local(src, dst):
        copy = pltpu.make_async_copy(src, dst, local_sem.at[new("local")])
        copy.start()
        return copy

    def lanes(h):
        return pl.ds(COLS * h, COLS)

    own = block_of(x, zl, core)
    own_in = [local(features.at[:, lanes(h)], slab[h].at[own]) for h in range(2)]
    meta_in = [local(block_rows, rows_s), local(block_cols, cols_s), local(block_count, count_s)]
    tiles_in = local(adjacency, tiles)
    dense_in = [local(weight, wgt), local(bias_term, bias), local(cotangent, cot)]

    peers = [at_x(v) for v in xs] + [at_zl(v) for v in zls] + [sibling] + [at_y(v) for v in ys] + [at_zh(v) for v in zhs]
    barrier = pltpu.get_barrier_semaphore()
    for peer in peers:
        pl.semaphore_signal(barrier, inc=1, device_id=peer, device_id_type=pl.DeviceIdType.MESH)
    pl.semaphore_wait(barrier, len(peers))

    f_sent = [new("send") for _ in range(2)]
    fz = [[new("recv") for _ in range(3)] for _ in range(2)]
    fx = [[new("recv") for _ in range(4)] for _ in range(2)]
    fc = [new("recv") for _ in range(2)]
    f_zl = (zl,) + zls

    def to_core(h, b):
        send(slab[h].at[b], slab[h].at[b], sibling, f_sent[h], fc[h])

    def to_x(h, c):
        b = block_of(x, f_zl[c], core)
        for v in xs:
            send(slab[h].at[b], slab[h].at[b], at_x(v), f_sent[h], fx[h][c])
        to_core(h, b)

    for h in range(2):
        own_in[h].wait()
        for i in range(3):
            send(slab[h].at[own], slab[h].at[own], at_zl(zls[i]), f_sent[h], fz[h][i])
        to_x(h, 0)
    for copy in meta_in:
        copy.wait()
    live = count_s[0, 0]
    chain[0] = jnp.zeros((BS, COLS), jnp.float32)
    chain_tables(rows_s, live, prev_f, last_f, TILE_ROWS)
    near_first = (2, 0, 1)
    for h in range(2):
        for i in near_first:
            arrived(fz[h][i], slab[h].at[0])
            to_x(h, i + 1)

    def feature_half(h):
        for c in (0, 3, 1, 2):
            arrived(fx[h][c], slab[h].at[pl.ds(0, 3)])
            for v in xs:
                to_core(h, block_of(v, f_zl[c], core))
        arrived(fc[h], slab[h].at[pl.ds(0, 16)])

    def products(h, source, source_ids, prev, dims):
        def some(g, carry):
            terms = []
            for j in range(GROUP):
                k = g * GROUP + j
                terms.append(
                    lax.dot_general(
                        tiles[k], source[h][source_ids[k]], (dims, ((), ())), preferred_element_type=jnp.float32
                    )
                )
            for j in range(GROUP):
                k = g * GROUP + j
                chain[k + 1] = terms[j] + chain[prev[k]]
            return carry

        lax.fori_loop(0, SLOTS // GROUP, some, 0, unroll=2)

    p_sent = [new("send") for _ in range(2)]
    py = [[new("recv") for _ in range(4)] for _ in range(2)]
    pz = [new("recv") for _ in range(2)]
    p_zh = zhs + (zh,)

    def partial_half(h):
        products(h, slab, cols_s, prev_f, ((1,), (0,)))
        for i in range(4):
            for v in ys:
                t = v * 4 + p_zh[i]
                part[h, t] = bf16(chain[last_f[t]])
            for j in range(3):
                t = ys[j] * 4 + p_zh[i]
                send(part.at[h, t], y_in.at[h, i, j], at_y(ys[j]), p_sent[h], py[h][i])
        for i in range(4):
            t = y * 4 + p_zh[i]
            part[h, t] = bf16(chain[last_f[t]])

    def partial_total(h):
        for i in range(4):
            arrived(py[h][i], y_in.at[h, 0])
            s = f32(part[h, y * 4 + p_zh[i]]) + f32(y_in[h, i, 0]) + f32(y_in[h, i, 1]) + f32(y_in[h, i, 2])
            mid[h, i] = bf16(s)
            if i < 3:
                send(mid.at[h, i], zh_in.at[h, i], at_zh(p_zh[i]), p_sent[h], pz[h])

    feature_half(0)
    tiles_in.wait()
    partial_half(0)
    feature_half(1)
    partial_half(1)
    partial_total(0)
    partial_total(1)
    chain_tables(cols_s, live, prev_b, last_b, TILE_COLS)
    for copy in dense_in:
        copy.wait()
    agg = []
    for h in range(2):
        arrived(pz[h], zh_in.at[h])
        agg.append(bf16(f32(mid[h, 3]) + f32(zh_in[h, 0]) + f32(zh_in[h, 1]) + f32(zh_in[h, 2])))

    pre = bias[...] + jnp.dot(agg[0], wgt[0:COLS, :], preferred_element_type=jnp.float32)
    pre = pre + jnp.dot(agg[1], wgt[COLS:H, :], preferred_element_type=jnp.float32)
    cdf = 0.5 * (1.0 + lax.erf(pre * INV_SQRT2))
    slope = cdf + pre * (jnp.exp(-0.5 * pre * pre) * INV_SQRT_2PI)
    grad_pre = bf16(f32(cot[...]) * slope)
    grad_agg = bf16(
        lax.dot_general(grad_pre, wgt[...], (((1,), (1,)), ((), ())), preferred_element_type=jnp.float32)
    )

    g_sent = [new("send") for _ in range(2)]
    gz = [[new("recv") for _ in range(3)] for _ in range(2)]
    gy = [[new("recv") for _ in range(4)] for _ in range(2)]
    g_zh = (zh, zhs[0], zhs[2], zhs[1])

    def to_y(h, i):
        b = y * 4 + g_zh[i]
        for v in ys:
            send(gslab[h].at[b], gslab[h].at[b], at_y(v), g_sent[h], gy[h][i])

    for h in range(2):
        gslab[h][col] = grad_agg[:, COLS * h : COLS * h + COLS]
        for i in range(3):
            send(gslab[h].at[col], gslab[h].at[col], at_zh(zhs[i]), g_sent[h], gz[h][i])
        to_y(h, 0)
    hid[...] = bf16(pre * cdf)
    hid_out = local(hid, hidden_out)

    w_sent = [new("send") for _ in range(8)]
    w_recv = [new("recv") for _ in range(8)]
    both = jnp.concatenate(agg, axis=1)
    grad_w = lax.dot_general(both, grad_pre, (((0,), (0,)), ((), ())), preferred_element_type=jnp.float32)
    w0[0, 0:128] = grad_w[0:128]
    w0[1, 0:128] = grad_w[128:256]
    grad_b = jnp.broadcast_to(jnp.sum(f32(grad_pre), axis=0, keepdims=True), (8, H))
    w0[0, 128:136] = grad_b
    w0[1, 128:136] = grad_b
    send(w0.at[other], w0_in, sibling, w_sent[0], w_recv[0])

    def weight_x():
        arrived(w_recv[0], w0_in)
        s = w0[core] + w0_in[...]
        for v in range(4):
            w1[v, 0:32] = s[32 * v : 32 * v + 32]
            w1[v, 32:40] = s[128:136]
        w1_in[x] = w1[x]
        for v in xs:
            send(w1.at[v], w1_in.at[x], at_x(v), w_sent[1], w_recv[1])

    def weight_zl():
        arrived(w_recv[1], w1_in.at[pl.ds(0, 3)])
        s = w1_in[0] + w1_in[1] + w1_in[2] + w1_in[3]
        for v in range(4):
            w2[v, 0:8] = s[8 * v : 8 * v + 8]
            w2[v, 8:16] = s[32:40]
        w2_in[zl] = w2[zl]
        for v in zls:
            send(w2.at[v], w2_in.at[zl], at_zl(v), w_sent[2], w_recv[2])

    def weight_y():
        arrived(w_recv[2], w2_in.at[pl.ds(0, 3)])
        w3_in[y] = w2_in[0] + w2_in[1] + w2_in[2] + w2_in[3]
        for v in ys:
            send(w3_in.at[y], w3_in.at[y], at_y(v), w_sent[3], w_recv[3])

    def weight_zh():
        arrived(w_recv[3], w3_in.at[pl.ds(0, 3)])
        w4_in[zh] = w3_in[0] + w3_in[1] + w3_in[2] + w3_in[3]
        for v in zhs:
            send(w4_in.at[zh], w4_in.at[zh], at_zh(v), w_sent[4], w_recv[4])

    mine = core * 16 + x * 4 + zl

    def weight_back_zl():
        arrived(w_recv[4], w4_in.at[pl.ds(0, 3)])
        s = (w4_in[0] + w4_in[1] + w4_in[2] + w4_in[3]) * (1.0 / math.sqrt(NODES))
        bfin[...] = s[8:9]
        wfin[mine] = s[0:8]
        for v in zls:
            send(wfin.at[mine], wfin.at[mine], at_zl(v), w_sent[5], w_recv[5])
        return local(bfin, bias_out)

    def weight_back_x():
        arrived(w_recv[5], wfin.at[pl.ds(0, 3)])
        quarter = pl.ds(core * 16 + x * 4, 4)
        for v in xs:
            send(wfin.at[quarter], wfin.at[quarter], at_x(v), w_sent[6], w_recv[6])

    def weight_back_core():
        arrived(w_recv[6], wfin.at[pl.ds(0, 12)])
        half = pl.ds(core * 16, 16)
        send(wfin.at[half], wfin.at[half], sibling, w_sent[7], w_recv[7])

    weight_x()
    for i in range(3):
        arrived(gz[0][i], gslab[0].at[0])
        to_y(0, i + 1)
    weight_zl()
    for i in range(3):
        arrived(gz[1][i], gslab[1].at[0])
        to_y(1, i + 1)
    weight_y()

    b_sent = [new("send") for _ in range(2)]
    bc = [[new("recv") for _ in range(4)] for _ in range(2)]
    bx = [[new("recv") for _ in range(4)] for _ in range(2)]
    bz = [new("recv") for _ in range(2)]
    b_zl = zls + (zl,)

    def back_half(h):
        for i in range(4):
            arrived(gy[h][i], gslab[h].at[pl.ds(0, 3)])
        products(h, gslab, rows_s, prev_b, ((0,), (0,)))
        for i in range(4):
            for v in xs + (x,):
                t = block_of(v, b_zl[i], other)
                back[h, t] = bf16(chain[last_b[t]])
            for v in xs + (x,):
                t = block_of(v, b_zl[i], other)
                send(back.at[h, t], core_in.at[h, v * 4 + b_zl[i]], sibling, b_sent[h], bc[h][i])
        for i in range(4):
            for v in xs + (x,):
                t = block_of(v, b_zl[i], core)
                back[h, t] = bf16(chain[last_b[t]])

    def core_total(h):
        for i in range(4):
            arrived(bc[h][i], core_in.at[h, pl.ds(0, 4)])
            for v in xs + (x,):
                q = v * 4 + b_zl[i]
                xsum[h, q] = bf16(f32(back[h, block_of(v, b_zl[i], core)]) + f32(core_in[h, q]))
            for j in range(3):
                send(xsum.at[h, xs[j] * 4 + b_zl[i]], x_in.at[h, i, j], at_x(xs[j]), b_sent[h], bx[h][i])

    def x_total(h):
        for i in range(4):
            arrived(bx[h][i], x_in.at[h, 0])
            s = f32(xsum[h, x * 4 + b_zl[i]]) + f32(x_in[h, i, 0]) + f32(x_in[h, i, 1]) + f32(x_in[h, i, 2])
            zl_out[h, i] = bf16(s)
            if i < 3:
                send(zl_out.at[h, i], zl_in.at[h, i], at_zl(b_zl[i]), b_sent[h], bz[h])

    def z_total(h):
        arrived(bz[h], zl_in.at[h])
        s = f32(zl_out[h, 3]) + f32(zl_in[h, 0]) + f32(zl_in[h, 1]) + f32(zl_in[h, 2])
        fin[h] = bf16(s)
        return local(fin.at[h], features_out.at[:, lanes(h)])

    back_half(0)
    core_total(0)
    weight_zh()
    back_half(1)
    core_total(1)
    x_total(0)
    b_out = weight_back_zl()
    x_total(1)
    weight_back_x()
    outs = [z_total(0)]
    weight_back_core()
    outs.append(z_total(1))
    arrived(w_recv[7], wfin.at[pl.ds(0, 16)])
    outs += [local(wfin, weight_out), hid_out, b_out]
    for h in range(2):
        left(f_sent[h], slab[h].at[pl.ds(0, 31)])
        left(p_sent[h], part.at[h, pl.ds(0, 15)])
        left(g_sent[h], gslab[h].at[pl.ds(0, 15)])
        left(b_sent[h], back.at[h, pl.ds(0, 31)])
    left(w_sent[0], w0_in)
    left(w_sent[1], w1_in.at[pl.ds(0, 3)])
    for i in (2, 3, 4):
        left(w_sent[i], w2_in.at[pl.ds(0, 3)])
    left(w_sent[5], wfin.at[pl.ds(0, 3)])
    left(w_sent[6], wfin.at[pl.ds(0, 12)])
    left(w_sent[7], wfin.at[pl.ds(0, 16)])
    for copy in outs:
        copy.wait()
    assert counts == {"send": SENDS, "recv": RECVS, "local": LOCALS}, counts


def write_kernel(hidden, weight, bias, features, hidden_out, weight_out, bias_out, features_out, h, w, b, f, sems):
    trios = ((features, f, features_out), (weight, w, weight_out), (hidden, h, hidden_out), (bias, b, bias_out))
    reads = [pltpu.make_async_copy(src, held, sems.at[i]) for i, (src, held, _) in enumerate(trios)]
    writes = [pltpu.make_async_copy(held, dst, sems.at[4 + i]) for i, (_, held, dst) in enumerate(trios)]
    for copy in reads:
        copy.start()
    for read, write in zip(reads, writes):
        read.wait()
        write.start()
    for copy in writes:
        copy.wait()


def shards(features, adjacency, block_rows, block_cols, block_count, weight, bias_term, cotangent):
    half, single = jnp.bfloat16, jnp.float32
    vmem = pltpu.VMEM
    hbm = pl.BlockSpec(memory_space=pl.ANY)
    scratch = [
        vmem((SLOTS, BS, BS), half),
        vmem((H, H), half),
        vmem((1, H), single),
        vmem((BS, H), half),
        vmem((SLOTS + 1, BS, COLS), single),
        vmem((TILE_COLS, BS, COLS), half),
        vmem((TILE_COLS, BS, COLS), half),
        vmem((2, TILE_ROWS, BS, COLS), half),
        vmem((2, 4, 3, BS, COLS), half),
        vmem((2, 4, BS, COLS), half),
        vmem((2, 3, BS, COLS), half),
        vmem((TILE_ROWS, BS, COLS), half),
        vmem((TILE_ROWS, BS, COLS), half),
        vmem((2, TILE_COLS, BS, COLS), half),
        vmem((2, 16, BS, COLS), half),
        vmem((2, 16, BS, COLS), half),
        vmem((2, 4, 3, BS, COLS), half),
        vmem((2, 4, BS, COLS), half),
        vmem((2, 3, BS, COLS), half),
        vmem((BS, H), half),
        vmem((2, BS, COLS), half),
        vmem((2, 136, H), single),
        vmem((136, H), single),
        vmem((4, 40, H), single),
        vmem((4, 40, H), single),
        vmem((4, 16, H), single),
        vmem((4, 16, H), single),
        vmem((4, 16, H), single),
        vmem((4, 16, H), single),
        vmem((32, 8, H), single),
        vmem((1, H), single),
        pltpu.SMEM((SLOTS,), jnp.int32),
        pltpu.SMEM((SLOTS,), jnp.int32),
        pltpu.SMEM((1, 1), jnp.int32),
        pltpu.SMEM((SLOTS,), jnp.int32),
        pltpu.SMEM((TILE_ROWS,), jnp.int32),
        pltpu.SMEM((SLOTS,), jnp.int32),
        pltpu.SMEM((TILE_COLS,), jnp.int32),
        pltpu.SemaphoreType.DMA((LOCALS,)),
        pltpu.SemaphoreType.DMA((SENDS,)),
        pltpu.SemaphoreType.DMA((RECVS,)),
    ]
    shapes = (
        jax.ShapeDtypeStruct((BS, H), half),
        jax.ShapeDtypeStruct((32, 8, H), single),
        jax.ShapeDtypeStruct((1, H), single),
        jax.ShapeDtypeStruct((BS, H), half),
    )
    results = pl.pallas_call(
        layer_kernel,
        out_shape=shapes,
        in_specs=[hbm] * 8,
        out_specs=(hbm,) * 4,
        scratch_shapes=scratch,
        compiler_params=pltpu.CompilerParams(
            collective_id=0, has_side_effects=True, vmem_limit_bytes=60 * 1024 * 1024
        ),
        name="gcn_layer",
    )(
        features,
        adjacency.reshape(SLOTS, BS, BS),
        block_rows.reshape(SLOTS),
        block_cols.reshape(SLOTS),
        block_count,
        weight,
        bias_term.reshape(1, H),
        cotangent,
    )
    hidden, grad_weight, grad_bias, grad_features = pl.pallas_call(
        write_kernel,
        out_shape=shapes,
        in_specs=[hbm] * 4,
        out_specs=(hbm,) * 4,
        scratch_shapes=[vmem(v.shape, v.dtype) for v in shapes] + [pltpu.SemaphoreType.DMA((8,))],
        compiler_params=pltpu.CompilerParams(vmem_limit_bytes=60 * 1024 * 1024),
        name="write_results",
    )(*results)
    return hidden, grad_weight.reshape(H, H), grad_bias.reshape(H), grad_features


def solution(mesh):
    return jax.shard_map(
        shards,
        mesh=mesh,
        in_specs=(
            P(("col", "row"), None),
            P("row", "col", None, None, None),
            P("row", "col", None),
            P("row", "col", None),
            P("row", "col"),
            P(),
            P(),
            P(("row", "col"), None),
        ),
        out_specs=(P(("row", "col"), None), P(), P(), P(("col", "row"), None)),
        check_vma=False,
    )
```

time: 962 us -> 94.9 us (0.10)
  waiting for transfers between devices: 635 us -> 0 us
  loops' own time: 121 us -> 0 us
  blocking collectives: 102 us -> 0 us
  Pallas kernels: 0 us -> 93.5 us
  other arithmetic: 62 us -> 0 us
  local copies, waits for them, and re-layouts: 12.8 us -> 0 us
  between operations: 13.9 us -> 1.29 us
    reduce_scatter x2 -> x0, waiting for transfers between devices: 258 us -> none  [the longest x1 147 us: shards(): lax.psum_scatter(back, 'row', scatter_dimension=0, tiled=True)]
    psum x1 -> x0, waiting for transfers between devices: 230 us -> none  [shards(): lax.psum((local_weight, local_bias), ('row', 'col'))]
    all_gather x2 -> x0, waiting for transfers between devices: 145 us -> none  [the longest x1 73.2 us: shards(): feature_slab = lax.all_gather(features, 'row', axis=0, tiled=True)]
    another operation x2 -> x0, loops' own time: 121 us -> none  [accumulate(): lax.fori_loop(0, last_step, advance, empty).reshape(-1, H)]
    psum x1 -> x0, blocking collectives: 102 us -> none  [shards(): lax.psum((local_weight, local_bias), ('row', 'col'))]
    pallas_call x0 -> x2, Pallas kernels: none -> 93.5 us  [the longest x1 91.7 us: shards(): pl.pallas_call(layer_kernel, out_shape=shapes, in_specs=[hbm] * 8, out_sp...]
    dynamic_update_slice x64 -> x0, other arithmetic: 51.3 us -> none  [advance(): lax.dynamic_update_slice_in_dim(running, current + products[slot][None],...]
  transfers between devices with their start and end apart: 5 -> 0, of which waited for: 5 -> 0; matrix products, arithmetic and copies ran while one was open for 7% -> 0% of each run, Pallas kernels for 0% -> 0%
where the time goes in v2:
time: 94.9 us; the launch traced here: 94.8 us
  Pallas kernels  93.5 us (99%)
  between operations  1.29 us (1%)
    pallas_call x1, Pallas kernels, shards(): pl.pallas_call(layer_kernel, out_shape=shapes, in_specs=[hbm] * 8, out_sp...  91.7 us

profile of v2, /device:TPU:1, one launch (start us, length us, event | category | flops | bytes accessed | tf_op | source)
XLA Modules:
  0.0 94.8 jit_solution(8385701062696934612)
XLA Ops:
  1.3 91.7 %gcn_layer.1 = (bf16[128,256]{1,0:T(8,128)(2,1)}, f32[32,8,256]{2,1,0:T(8,128)}, f32[1,256]{1,0:T(1,128)}, bf16[128,256]{1,0:T(8,128)(2,1)}) custom-call(bf16[128,256]{1,0:T(8,128)(2,1)} %features.1, bf16[32,128,128]{2,1,0:T(8,128)(2,1)} %bitcast.6, s32[32]{0:T(128)} %bitcast.8, s32[32]{0:T(128)} %bitcast.9, s32[1,1]{1,0:T(1,128)S(6)} %copy.12.block_count, ...), custom_call_target="tpu_custom_call" | custom-call | tf_op jit(solution)/shard_map/gcn_layer/pallas_call | solution.py:474
  93.0 1.8 %write_results.1 = (bf16[128,256]{1,0:T(8,128)(2,1)}, f32[32,8,256]{2,1,0:T(8,128)}, f32[1,256]{1,0:T(1,128)}, bf16[128,256]{1,0:T(8,128)(2,1)}) custom-call(bf16[128,256]{1,0:T(8,128)(2,1)} %get-tuple-element.12.hidden, f32[32,8,256]{2,1,0:T(8,128)} %get-tuple-element.13.weight, f32[1,256]{1,0:T(1,128)} %get-tuple-element.14.bias, ...), custom_call_target="tpu_custom_call" | custom-call | tf_op jit(solution)/shard_map/write_results/pallas_call | solution.py:494

commit v3 on v2

--- a/solution.py
+++ b/solution.py
@@ -56,7 +56,7 @@
     features, adjacency, block_rows, block_cols, block_count, weight, bias_term, cotangent,
     hidden_out, weight_out, bias_out, features_out,
     tiles, wgt, bias, cot, chain, slab_a, slab_b, part, y_in, mid, zh_in, gslab_a, gslab_b, back, core_in, xsum, x_in, zl_out, zl_in,
-    hid, fin, w0, w0_in, w1, w1_in, w2, w2_in, w3_in, w4_in, wfin, bfin,
+    hid, fin, w0, w0_in, w1, w1_in, w2_in, w3, w3_in, w4_in, wfin, bfin,
     rows_s, cols_s, count_s, prev_f, last_f, prev_b, last_b,
     local_sem, send_sem, recv_sem,
 ):
@@ -125,7 +125,7 @@
     tiles_in = local(adjacency, tiles)
     dense_in = [local(weight, wgt), local(bias_term, bias), local(cotangent, cot)]
 
-    peers = [at_x(v) for v in xs] + [at_zl(v) for v in zls] + [sibling] + [at_y(v) for v in ys] + [at_zh(v) for v in zhs]
+    peers = [at_zh(v) for v in zhs] + [at_zl(v) for v in zls] + [at_x(v) for v in xs] + [at_y(v) for v in ys] + [sibling]
     barrier = pltpu.get_barrier_semaphore()
     for peer in peers:
         pl.semaphore_signal(barrier, inc=1, device_id=peer, device_id_type=pl.DeviceIdType.MESH)
@@ -146,21 +146,27 @@
             send(slab[h].at[b], slab[h].at[b], at_x(v), f_sent[h], fx[h][c])
         to_core(h, b)
 
-    for h in range(2):
-        own_in[h].wait()
+    def to_zl(h):
         for i in range(3):
             send(slab[h].at[own], slab[h].at[own], at_zl(zls[i]), f_sent[h], fz[h][i])
-        to_x(h, 0)
+
+    own_in[0].wait()
+    to_zl(0)
+    to_x(0, 0)
+    own_in[1].wait()
+    to_x(1, 0)
     for copy in meta_in:
         copy.wait()
     live = count_s[0, 0]
     chain[0] = jnp.zeros((BS, COLS), jnp.float32)
-    chain_tables(rows_s, live, prev_f, last_f, TILE_ROWS)
     near_first = (2, 0, 1)
     for h in range(2):
         for i in near_first:
             arrived(fz[h][i], slab[h].at[0])
             to_x(h, i + 1)
+            if (h, i) == (0, 2):
+                to_zl(1)
+    chain_tables(rows_s, live, prev_f, last_f, TILE_ROWS)
 
     def feature_half(h):
         for c in (0, 3, 1, 2):
@@ -186,37 +192,53 @@
 
         lax.fori_loop(0, SLOTS // GROUP, some, 0, unroll=2)
 
+    class Ring:
+        def __init__(self, h, to, at, source, sent, into):
+            self.h, self.to, self.at, self.source, self.sent, self.into = h, to, at, source, sent, into
+            self.sem = [new("recv") for _ in range(4)]
+
+        def terms(self, i):
+            for j in range(3):
+                v = self.to[j]
+                send(self.source(v, i), self.into.at[self.h, i, j], self.at(v), self.sent, self.sem[i])
+
+        def total(self, i, own_term):
+            arrived(self.sem[i], self.into.at[self.h, i])
+            s = f32(own_term)
+            for j in range(3):
+                s = s + f32(self.into[self.h, i, j])
+            return bf16(s)
+
     p_sent = [new("send") for _ in range(2)]
-    py = [[new("recv") for _ in range(4)] for _ in range(2)]
+    p_zh = zhs + (zh,)
+    p_ring = [
+        Ring(h, ys, at_y, lambda v, i, h=h: part.at[h, v * 4 + p_zh[i]], p_sent[h], y_in)
+        for h in range(2)
+    ]
     pz = [new("recv") for _ in range(2)]
-    p_zh = zhs + (zh,)
-
-    def partial_half(h):
-        products(h, slab, cols_s, prev_f, ((1,), (0,)))
-        for i in range(4):
-            for v in ys:
-                t = v * 4 + p_zh[i]
-                part[h, t] = bf16(chain[last_f[t]])
-            for j in range(3):
-                t = ys[j] * 4 + p_zh[i]
-                send(part.at[h, t], y_in.at[h, i, j], at_y(ys[j]), p_sent[h], py[h][i])
-        for i in range(4):
-            t = y * 4 + p_zh[i]
+
+    def partial_place(h, i):
+        for v in ys + (y,):
+            t = v * 4 + p_zh[i]
             part[h, t] = bf16(chain[last_f[t]])
 
     def partial_total(h):
         for i in range(4):
-            arrived(py[h][i], y_in.at[h, 0])
-            s = f32(part[h, y * 4 + p_zh[i]]) + f32(y_in[h, i, 0]) + f32(y_in[h, i, 1]) + f32(y_in[h, i, 2])
-            mid[h, i] = bf16(s)
+            mid[h, i] = p_ring[h].total(i, part[h, y * 4 + p_zh[i]])
             if i < 3:
                 send(mid.at[h, i], zh_in.at[h, i], at_zh(p_zh[i]), p_sent[h], pz[h])
 
     feature_half(0)
     tiles_in.wait()
-    partial_half(0)
+    products(0, slab, cols_s, prev_f, ((1,), (0,)))
+    for i in range(4):
+        partial_place(0, i)
+        p_ring[0].terms(i)
     feature_half(1)
-    partial_half(1)
+    products(1, slab, cols_s, prev_f, ((1,), (0,)))
+    for i in range(4):
+        partial_place(1, i)
+        p_ring[1].terms(i)
     partial_total(0)
     partial_total(1)
     chain_tables(cols_s, live, prev_b, last_b, TILE_COLS)
@@ -246,10 +268,14 @@
         for v in ys:
             send(gslab[h].at[b], gslab[h].at[b], at_y(v), g_sent[h], gy[h][i])
 
+    def to_zh(h, i):
+        send(gslab[h].at[col], gslab[h].at[col], at_zh(zhs[i]), g_sent[h], gz[h][i])
+
     for h in range(2):
         gslab[h][col] = grad_agg[:, COLS * h : COLS * h + COLS]
-        for i in range(3):
-            send(gslab[h].at[col], gslab[h].at[col], at_zh(zhs[i]), g_sent[h], gz[h][i])
+        if h == 0:
+            for i in (1, 2, 0):
+                to_zh(0, i)
         to_y(h, 0)
     hid[...] = bf16(pre * cdf)
     hid_out = local(hid, hidden_out)
@@ -275,21 +301,21 @@
         for v in xs:
             send(w1.at[v], w1_in.at[x], at_x(v), w_sent[1], w_recv[1])
 
+    def weight_y():
+        arrived(w_recv[1], w1_in.at[pl.ds(0, 3)])
+        w2_in[y] = w1_in[0] + w1_in[1] + w1_in[2] + w1_in[3]
+        for v in ys:
+            send(w2_in.at[y], w2_in.at[y], at_y(v), w_sent[2], w_recv[2])
+
     def weight_zl():
-        arrived(w_recv[1], w1_in.at[pl.ds(0, 3)])
-        s = w1_in[0] + w1_in[1] + w1_in[2] + w1_in[3]
+        arrived(w_recv[2], w2_in.at[pl.ds(0, 3)])
+        s = w2_in[0] + w2_in[1] + w2_in[2] + w2_in[3]
         for v in range(4):
-            w2[v, 0:8] = s[8 * v : 8 * v + 8]
-            w2[v, 8:16] = s[32:40]
-        w2_in[zl] = w2[zl]
+            w3[v, 0:8] = s[8 * v : 8 * v + 8]
+            w3[v, 8:16] = s[32:40]
+        w3_in[zl] = w3[zl]
         for v in zls:
-            send(w2.at[v], w2_in.at[zl], at_zl(v), w_sent[2], w_recv[2])
-
-    def weight_y():
-        arrived(w_recv[2], w2_in.at[pl.ds(0, 3)])
-        w3_in[y] = w2_in[0] + w2_in[1] + w2_in[2] + w2_in[3]
-        for v in ys:
-            send(w3_in.at[y], w3_in.at[y], at_y(v), w_sent[3], w_recv[3])
+            send(w3.at[v], w3_in.at[zl], at_zl(v), w_sent[3], w_recv[3])
 
     def weight_zh():
         arrived(w_recv[3], w3_in.at[pl.ds(0, 3)])
@@ -319,21 +345,29 @@
         half = pl.ds(core * 16, 16)
         send(wfin.at[half], wfin.at[half], sibling, w_sent[7], w_recv[7])
 
+    def gradient_relay(h, i):
+        arrived(gz[h][i], gslab[h].at[0])
+        to_y(h, i + 1)
+
     weight_x()
-    for i in range(3):
-        arrived(gz[0][i], gslab[0].at[0])
-        to_y(0, i + 1)
+    weight_y()
+    for i in (1, 2, 0):
+        to_zh(1, i)
+    for i in (1, 2, 0):
+        gradient_relay(0, i)
     weight_zl()
-    for i in range(3):
-        arrived(gz[1][i], gslab[1].at[0])
-        to_y(1, i + 1)
-    weight_y()
+    for i in (1, 2, 0):
+        gradient_relay(1, i)
+    weight_zh()
 
     b_sent = [new("send") for _ in range(2)]
     bc = [[new("recv") for _ in range(4)] for _ in range(2)]
-    bx = [[new("recv") for _ in range(4)] for _ in range(2)]
     bz = [new("recv") for _ in range(2)]
     b_zl = zls + (zl,)
+    b_ring = [
+        Ring(h, xs, at_x, lambda v, i, h=h: xsum.at[h, v * 4 + b_zl[i]], b_sent[h], x_in)
+        for h in range(2)
+    ]
 
     def back_half(h):
         for i in range(4):
@@ -351,22 +385,16 @@
                 t = block_of(v, b_zl[i], core)
                 back[h, t] = bf16(chain[last_b[t]])
 
-    def core_total(h):
-        for i in range(4):
-            arrived(bc[h][i], core_in.at[h, pl.ds(0, 4)])
-            for v in xs + (x,):
-                q = v * 4 + b_zl[i]
-                xsum[h, q] = bf16(f32(back[h, block_of(v, b_zl[i], core)]) + f32(core_in[h, q]))
-            for j in range(3):
-                send(xsum.at[h, xs[j] * 4 + b_zl[i]], x_in.at[h, i, j], at_x(xs[j]), b_sent[h], bx[h][i])
-
-    def x_total(h):
-        for i in range(4):
-            arrived(bx[h][i], x_in.at[h, 0])
-            s = f32(xsum[h, x * 4 + b_zl[i]]) + f32(x_in[h, i, 0]) + f32(x_in[h, i, 1]) + f32(x_in[h, i, 2])
-            zl_out[h, i] = bf16(s)
-            if i < 3:
-                send(zl_out.at[h, i], zl_in.at[h, i], at_zl(b_zl[i]), b_sent[h], bz[h])
+    def core_total(h, i):
+        arrived(bc[h][i], core_in.at[h, pl.ds(0, 4)])
+        for v in xs + (x,):
+            q = v * 4 + b_zl[i]
+            xsum[h, q] = bf16(f32(back[h, block_of(v, b_zl[i], core)]) + f32(core_in[h, q]))
+
+    def x_total(h, i):
+        zl_out[h, i] = b_ring[h].total(i, xsum[h, x * 4 + b_zl[i]])
+        if i < 3:
+            send(zl_out.at[h, i], zl_in.at[h, i], at_zl(b_zl[i]), b_sent[h], bz[h])
 
     def z_total(h):
         arrived(bz[h], zl_in.at[h])
@@ -375,14 +403,21 @@
         return local(fin.at[h], features_out.at[:, lanes(h)])
 
     back_half(0)
-    core_total(0)
-    weight_zh()
+    for i in range(4):
+        core_total(0, i)
+        b_ring[0].terms(i)
     back_half(1)
-    core_total(1)
-    x_total(0)
+    for i in range(4):
+        core_total(1, i)
+        b_ring[1].terms(i)
+    for i in range(4):
+        x_total(0, i)
     b_out = weight_back_zl()
-    x_total(1)
+    x_total(1, 0)
+    x_total(1, 1)
     weight_back_x()
+    x_total(1, 2)
+    x_total(1, 3)
     outs = [z_total(0)]
     weight_back_core()
     outs.append(z_total(1))
@@ -395,8 +430,9 @@
         left(b_sent[h], back.at[h, pl.ds(0, 31)])
     left(w_sent[0], w0_in)
     left(w_sent[1], w1_in.at[pl.ds(0, 3)])
-    for i in (2, 3, 4):
-        left(w_sent[i], w2_in.at[pl.ds(0, 3)])
+    left(w_sent[2], w2_in.at[pl.ds(0, 3)])
+    left(w_sent[3], w3_in.at[pl.ds(0, 3)])
+    left(w_sent[4], w4_in.at[pl.ds(0, 3)])
     left(w_sent[5], wfin.at[pl.ds(0, 3)])
     left(w_sent[6], wfin.at[pl.ds(0, 12)])
     left(w_sent[7], wfin.at[pl.ds(0, 16)])
@@ -448,7 +484,7 @@
         vmem((136, H), single),
         vmem((4, 40, H), single),
         vmem((4, 40, H), single),
-        vmem((4, 16, H), single),
+        vmem((4, 40, H), single),
         vmem((4, 16, H), single),
         vmem((4, 16, H), single),
         vmem((4, 16, H), single),

time: 94.9 us -> 91.4 us (0.963)
  Pallas kernels: 93.5 us -> 90 us
    pallas_call x1, Pallas kernels: 91.7 us -> 88.2 us  [shards(): pl.pallas_call(layer_kernel, out_shape=shapes, in_specs=[hbm] * 8, out_sp...]
where the time goes in v3:
time: 91.4 us; the launch traced here: 91.3 us
  Pallas kernels  90 us (98%)
  between operations  1.29 us (1%)
    pallas_call x1, Pallas kernels, shards(): pl.pallas_call(layer_kernel, out_shape=shapes, in_specs=[hbm] * 8, out_sp...  88.2 us

profile of v3, /device:TPU:1, one launch (start us, length us, event | category | flops | bytes accessed | tf_op | source)
XLA Modules:
  0.0 91.3 jit_solution(13246539760498775644)
XLA Ops:
  1.3 88.2 %gcn_layer.1 = (bf16[128,256]{1,0:T(8,128)(2,1)}, f32[32,8,256]{2,1,0:T(8,128)}, f32[1,256]{1,0:T(1,128)}, bf16[128,256]{1,0:T(8,128)(2,1)}) custom-call(bf16[128,256]{1,0:T(8,128)(2,1)} %features.1, bf16[32,128,128]{2,1,0:T(8,128)(2,1)} %bitcast.6, s32[32]{0:T(128)} %bitcast.8, s32[32]{0:T(128)} %bitcast.9, s32[1,1]{1,0:T(1,128)S(6)} %copy.12.block_count, ...), custom_call_target="tpu_custom_call" | custom-call | tf_op jit(solution)/shard_map/gcn_layer/pallas_call | solution.py:510
  89.5 1.8 %write_results.1 = (bf16[128,256]{1,0:T(8,128)(2,1)}, f32[32,8,256]{2,1,0:T(8,128)}, f32[1,256]{1,0:T(1,128)}, bf16[128,256]{1,0:T(8,128)(2,1)}) custom-call(bf16[128,256]{1,0:T(8,128)(2,1)} %get-tuple-element.12.hidden, f32[32,8,256]{2,1,0:T(8,128)} %get-tuple-element.13.weight, f32[1,256]{1,0:T(1,128)} %get-tuple-element.14.bias, ...), custom_call_target="tpu_custom_call" | custom-call | tf_op jit(solution)/shard_map/write_results/pallas_call | solution.py:530

commit v4 on v3

--- a/solution.py
+++ b/solution.py
@@ -349,17 +349,6 @@
         arrived(gz[h][i], gslab[h].at[0])
         to_y(h, i + 1)
 
-    weight_x()
-    weight_y()
-    for i in (1, 2, 0):
-        to_zh(1, i)
-    for i in (1, 2, 0):
-        gradient_relay(0, i)
-    weight_zl()
-    for i in (1, 2, 0):
-        gradient_relay(1, i)
-    weight_zh()
-
     b_sent = [new("send") for _ in range(2)]
     bc = [[new("recv") for _ in range(4)] for _ in range(2)]
     bz = [new("recv") for _ in range(2)]
@@ -402,22 +391,32 @@
         fin[h] = bf16(s)
         return local(fin.at[h], features_out.at[:, lanes(h)])
 
+    def core_half(h):
+        for i in range(4):
+            core_total(h, i)
+            b_ring[h].terms(i)
+
+    weight_x()
+    weight_y()
+    for i in (1, 2, 0):
+        to_zh(1, i)
+    for i in (1, 2, 0):
+        gradient_relay(0, i)
+    weight_zl()
+    gradient_relay(1, 1)
+    gradient_relay(1, 2)
+    weight_zh()
     back_half(0)
-    for i in range(4):
-        core_total(0, i)
-        b_ring[0].terms(i)
+    gradient_relay(1, 0)
+    core_half(0)
     back_half(1)
-    for i in range(4):
-        core_total(1, i)
-        b_ring[1].terms(i)
+    core_half(1)
+    b_out = weight_back_zl()
     for i in range(4):
         x_total(0, i)
-    b_out = weight_back_zl()
-    x_total(1, 0)
-    x_total(1, 1)
     weight_back_x()
-    x_total(1, 2)
-    x_total(1, 3)
+    for i in range(4):
+        x_total(1, i)
     outs = [z_total(0)]
     weight_back_core()
     outs.append(z_total(1))

time: 91.4 us -> 88.3 us (0.966)
  Pallas kernels: 90 us -> 86.8 us
    pallas_call x1, Pallas kernels: 88.2 us -> 85.1 us  [shards(): pl.pallas_call(layer_kernel, out_shape=shapes, in_specs=[hbm] * 8, out_sp...]
where the time goes in v4:
time: 88.3 us; the launch traced here: 88.1 us
  Pallas kernels  86.8 us (98%)
  between operations  1.29 us (1%)
    pallas_call x1, Pallas kernels, shards(): pl.pallas_call(layer_kernel, out_shape=shapes, in_specs=[hbm] * 8, out_sp...  85.1 us
    pallas_call x1, Pallas kernels, shards(): pl.pallas_call(write_kernel, out_shape=shapes, in_specs=[hbm] * 4, out_sp...  1.78 us

profile of v4, /device:TPU:1, one launch (start us, length us, event | category | flops | bytes accessed | tf_op | source)
XLA Modules:
  0.0 88.1 jit_solution(17995875090084562593)
XLA Ops:
  1.3 85.1 %gcn_layer.1 = (bf16[128,256]{1,0:T(8,128)(2,1)}, f32[32,8,256]{2,1,0:T(8,128)}, f32[1,256]{1,0:T(1,128)}, bf16[128,256]{1,0:T(8,128)(2,1)}) custom-call(bf16[128,256]{1,0:T(8,128)(2,1)} %features.1, bf16[32,128,128]{2,1,0:T(8,128)(2,1)} %bitcast.6, s32[32]{0:T(128)} %bitcast.8, s32[32]{0:T(128)} %bitcast.9, s32[1,1]{1,0:T(1,128)S(6)} %copy.12.block_count, ...), custom_call_target="tpu_custom_call" | custom-call | tf_op jit(solution)/shard_map/gcn_layer/pallas_call | solution.py:509
  86.4 1.8 %write_results.1 = (bf16[128,256]{1,0:T(8,128)(2,1)}, f32[32,8,256]{2,1,0:T(8,128)}, f32[1,256]{1,0:T(1,128)}, bf16[128,256]{1,0:T(8,128)(2,1)}) custom-call(bf16[128,256]{1,0:T(8,128)(2,1)} %get-tuple-element.12.hidden, f32[32,8,256]{2,1,0:T(8,128)} %get-tuple-element.13.weight, f32[1,256]{1,0:T(1,128)} %get-tuple-element.14.bias, ...), custom_call_target="tpu_custom_call" | custom-call | tf_op jit(solution)/shard_map/write_results/pallas_call | solution.py:529

commit v5 on v4

--- a/solution.py
+++ b/solution.py
@@ -55,7 +55,7 @@
 def layer_kernel(
     features, adjacency, block_rows, block_cols, block_count, weight, bias_term, cotangent,
     hidden_out, weight_out, bias_out, features_out,
-    tiles, wgt, bias, cot, chain, slab_a, slab_b, part, y_in, mid, zh_in, gslab_a, gslab_b, back, core_in, xsum, x_in, zl_out, zl_in,
+    tiles, turned, wgt, bias, cot, chain, slab_a, slab_b, part, y_in, mid, zh_in, gslab_a, gslab_b, back, core_in, xsum, x_in, zl_out, zl_in,
     hid, fin, w0, w0_in, w1, w1_in, w2_in, w3, w3_in, w4_in, wfin, bfin,
     rows_s, cols_s, count_s, prev_f, last_f, prev_b, last_b,
     local_sem, send_sem, recv_sem,
@@ -175,22 +175,20 @@
                 to_core(h, block_of(v, f_zl[c], core))
         arrived(fc[h], slab[h].at[pl.ds(0, 16)])
 
-    def products(h, source, source_ids, prev, dims):
+    def products(h, table, source, source_ids, prev):
         def some(g, carry):
             terms = []
             for j in range(GROUP):
                 k = g * GROUP + j
                 terms.append(
-                    lax.dot_general(
-                        tiles[k], source[h][source_ids[k]], (dims, ((), ())), preferred_element_type=jnp.float32
-                    )
+                    jnp.dot(table[k], source[h][source_ids[k]], preferred_element_type=jnp.float32)
                 )
             for j in range(GROUP):
                 k = g * GROUP + j
                 chain[k + 1] = terms[j] + chain[prev[k]]
             return carry
 
-        lax.fori_loop(0, SLOTS // GROUP, some, 0, unroll=2)
+        lax.fori_loop(0, SLOTS // GROUP, some, 0, unroll=4)
 
     class Ring:
         def __init__(self, h, to, at, source, sent, into):
@@ -230,15 +228,20 @@
 
     feature_half(0)
     tiles_in.wait()
-    products(0, slab, cols_s, prev_f, ((1,), (0,)))
+    products(0, tiles, slab, cols_s, prev_f)
     for i in range(4):
         partial_place(0, i)
         p_ring[0].terms(i)
     feature_half(1)
-    products(1, slab, cols_s, prev_f, ((1,), (0,)))
+    products(1, tiles, slab, cols_s, prev_f)
     for i in range(4):
         partial_place(1, i)
         p_ring[1].terms(i)
+    def turn(k, carry):
+        turned[k] = tiles[k].T
+        return carry
+
+    lax.fori_loop(0, SLOTS, turn, 0, unroll=4)
     partial_total(0)
     partial_total(1)
     chain_tables(cols_s, live, prev_b, last_b, TILE_COLS)
@@ -361,7 +364,7 @@
     def back_half(h):
         for i in range(4):
             arrived(gy[h][i], gslab[h].at[pl.ds(0, 3)])
-        products(h, gslab, rows_s, prev_b, ((0,), (0,)))
+        products(h, turned, gslab, rows_s, prev_b)
         for i in range(4):
             for v in xs + (x,):
                 t = block_of(v, b_zl[i], other)
@@ -458,6 +461,7 @@
     vmem = pltpu.VMEM
     hbm = pl.BlockSpec(memory_space=pl.ANY)
     scratch = [
+        vmem((SLOTS, BS, BS), half),
         vmem((SLOTS, BS, BS), half),
         vmem((H, H), half),
         vmem((1, H), single),

time: 88.3 us -> 87.7 us (level)
  no operation moved by 1% of the time
where the time goes in v5:
time: 87.7 us; the launch traced here: 88.1 us
  Pallas kernels  86.8 us (99%)
  between operations  1.29 us (1%)
    pallas_call x1, Pallas kernels, shards(): pl.pallas_call(layer_kernel, out_shape=shapes, in_specs=[hbm] * 8, out_sp...  85 us
    pallas_call x1, Pallas kernels, shards(): pl.pallas_call(write_kernel, out_shape=shapes, in_specs=[hbm] * 4, out_sp...  1.78 us

profile of v5, /device:TPU:1, one launch (start us, length us, event | category | flops | bytes accessed | tf_op | source)
XLA Modules:
  0.0 88.1 jit_solution(8067718868719825530)
XLA Ops:
  1.3 85.0 %gcn_layer.1 = (bf16[128,256]{1,0:T(8,128)(2,1)}, f32[32,8,256]{2,1,0:T(8,128)}, f32[1,256]{1,0:T(1,128)}, bf16[128,256]{1,0:T(8,128)(2,1)}) custom-call(bf16[128,256]{1,0:T(8,128)(2,1)} %features.1, bf16[32,128,128]{2,1,0:T(8,128)(2,1)} %bitcast.6, s32[32]{0:T(128)} %bitcast.8, s32[32]{0:T(128)} %bitcast.9, s32[1,1]{1,0:T(1,128)S(6)} %copy.12.block_count, ...), custom_call_target="tpu_custom_call" | custom-call | tf_op jit(solution)/shard_map/gcn_layer/pallas_call | solution.py:513
  86.3 1.8 %write_results.1 = (bf16[128,256]{1,0:T(8,128)(2,1)}, f32[32,8,256]{2,1,0:T(8,128)}, f32[1,256]{1,0:T(1,128)}, bf16[128,256]{1,0:T(8,128)(2,1)}) custom-call(bf16[128,256]{1,0:T(8,128)(2,1)} %get-tuple-element.12.hidden, f32[32,8,256]{2,1,0:T(8,128)} %get-tuple-element.13.weight, f32[1,256]{1,0:T(1,128)} %get-tuple-element.14.bias, ...), custom_call_target="tpu_custom_call" | custom-call | tf_op jit(solution)/shard_map/write_results/pallas_call | solution.py:533
